TPU v7x, 32 devices: a whole 2x2x4 slice. The times are simulated.
32 devices in a mesh: groups: 2 (over y), tmpl: 4 (over z), chan: 2 (over x), tm: 2 (over core).
Axes of the slice: x: 2, y: 2, z: 4, core: 2. Of those that a mesh axis runs over, the one named last changes fastest.
Arguments:
- samples: bfloat16 [1792, 3584], P(('tmpl', 'chan'), ('groups', 'tm')), parts along dimension 1, may hold values from -6 to 6
- tail: bfloat16 [1792, 1792], P(('tmpl', 'chan'), 'groups'), parts along dimension 1, may hold values from -6 to 6
- templates: bfloat16 [128, 8, 640], P('tmpl', 'chan'), may hold values from -6 to 6
- channels: int32 [128, 8], P('tmpl', 'chan'), may hold values from 0 to 1791
- moveouts: int32 [128, 8], P('tmpl', 'chan'), may hold values from 0 to 256
- live: int32 [128], P('tmpl'), may hold values from 4 to 8
Outputs:
- detection: float32 [128, 3584], P(('tmpl', 'chan'), ('groups', 'tm')), parts along dimension 1
There are 2 independent parts, one for each index of `groups`. A program takes and returns all parts, laid end to end along the dimension named above; an argument that names none is the same for every part. Nothing has to cross between parts.
All inputs are finite; a program needn't handle non-finite values.
Results may differ from a plain program's by a relative error of at most 0.0003.
Values may be sent and summed in bfloat16 or wider, within the bound.
A program may use at most 64 MiB of HBM per device.

v0:
```python
import jax
import jax.numpy as jnp
from jax import lax
from jax.sharding import PartitionSpec as P

EPS = 1e-06


def shifted(block, axis, distance):
    devices = range(lax.axis_size(axis))
    route = [(i - distance, i) for i in devices if i - distance in devices]
    return lax.ppermute(block, axis, route)


def depthwise(signal, kernel):
    output = lax.conv_general_dilated(
        signal[None],
        kernel[:, None, :],
        (1,),
        "VALID",
        dimension_numbers=("NCH", "OIH", "NCH"),
        feature_group_count=signal.shape[0],
        precision=None,
        preferred_element_type=jnp.float32,
    )
    return output[0]


def shifted_rows(window, chan_ids, offsets, length):
    picked = jnp.take(window, chan_ids, axis=0)

    def one_row(row_data, offset):
        return lax.dynamic_slice_in_dim(row_data, offset, length)

    return jax.vmap(one_row)(picked, offsets)


def running_energy(squares, length):
    totals = jnp.cumsum(squares, axis=1)
    totals = jnp.concatenate([jnp.zeros((squares.shape[0], 1), jnp.float32), totals], axis=1)
    return totals[:, length:] - totals[:, : totals.shape[1] - length]


def body(samples, tail, templates, channels, moveouts, live):
    block = samples.shape[1]
    length = templates.shape[2]
    per_dev = templates.shape[0]
    per_slot = templates.shape[1]
    is_last = lax.axis_index("tm") == lax.axis_size("tm") - 1
    gathered, tail_all = (
        lax.all_gather(samples, ("tmpl", "chan"), axis=0, tiled=True),
        lax.all_gather(tail, ("tmpl", "chan"), axis=0, tiled=True),
    )
    following = shifted(gathered, "tm", -1)
    rim_all = jnp.where(is_last, tail_all, following)
    window = jnp.concatenate([gathered, rim_all], axis=1)
    slots = per_dev * per_slot
    chan_ids = channels.reshape(slots)
    offsets = moveouts.reshape(slots)
    waveform = templates.reshape(slots, length)
    slot_data = shifted_rows(window, chan_ids, offsets, block + length)
    correlation = depthwise(slot_data, waveform)[:, :block]
    squares = slot_data.astype(jnp.float32) ** 2
    energy = running_energy(squares, length)[:, :block]
    tnorm = jnp.sqrt(jnp.sum(waveform.astype(jnp.float32) ** 2, axis=-1) + EPS)
    ncc = correlation / (tnorm[:, None] * jnp.sqrt(energy + EPS))
    slot_index = lax.axis_index("chan") * per_slot + jnp.arange(per_slot)
    used_f = live.astype(jnp.float32)
    weight = jnp.where(
        slot_index[None, :] < live[:, None],
        jnp.sqrt(jnp.float32(length) / used_f)[:, None],
        jnp.float32(0.0),
    )
    partial_value = jnp.sum(weight[:, :, None] * ncc.reshape(per_dev, per_slot, block), axis=1)
    return lax.psum_scatter(partial_value, "chan", scatter_dimension=0, tiled=True)


def solution(mesh):
    in_specs = (
        P(("tmpl", "chan"), ("groups", "tm")),
        P(("tmpl", "chan"), "groups"),
        P("tmpl", "chan", None),
        P("tmpl", "chan"),
        P("tmpl", "chan"),
        P("tmpl"),
    )
    out_specs = P(("tmpl", "chan"), ("groups", "tm"))
    return jax.shard_map(body, mesh=mesh, in_specs=in_specs, out_specs=out_specs, check_vma=False)
```

profile of v0, /device:TPU:0, one launch (start us, length us, event | category | flops | bytes accessed | tf_op | source)
XLA Modules:
  0.0 500.3 jit_solution(5744314067343996593)
XLA Ops:
  8.1 65.3 %all-gather.3.cloned.1.call-done = bf16[1792,896]{1,0:T(8,128)(2,1)} async-done(((bf16[224,896]{1,0:T(8,128)(2,1)}), bf16[1792,896]{1,0:T(8,128)(2,1)}) %all-gather.3.cloned.1.call-update) | async-done | bytes 3211280 | tf_op jit(solution)/shard_map/all_gather | solution.py:51
  82.5 52.7 %all-gather.5.cloned.1.call-done = bf16[1792,896]{1,0:T(8,128)(2,1)} async-done(((bf16[224,896]{1,0:T(8,128)(2,1)}), bf16[1792,896]{1,0:T(8,128)(2,1)}) %all-gather.5.cloned.1.call-update) | async-done | bytes 3211280 | tf_op jit(solution)/shard_map/all_gather | solution.py:52
  135.2 2.3 broadcast_select_fusion
  137.5 3.1 pad_maximum_fusion
  140.7 5.2 %gather_fusion = bf16[128,1792]{1,0:T(8,128)(2,1)S(1)} fusion(bf16[1792,1792]{1,0:T(8,128)(2,1)} %pad_maximum_fusion, s32[1024]{0:T(1024)} %pad_clamp_fusion), kind=kCustom, calls=%fused_computation | custom fusion | bytes 918016 | tf_op jit(solution)/shard_map/jit(_take)/gather | solution.py:30
  146.0 264.2 %while.1 = (s32[]{:T(128)}, bf16[128,1792]{1,0:T(8,128)(2,1)S(1)}, s32[128,2]{0,1:T(2,128)S(1)}, bf16[128,1536]{1,0:T(8,128)(2,1)S(1)}, s32[]{:T(128)}, /*index=5*/s32[]{:T(128)}) while((s32[]{:T(128)}, bf16[128,1792]{1,0:T(8,128)(2,1)S(1)}, s32[128,2]{0,1:T(2,128)S(1)}, bf16[128,1536]{1,0:T(8,128)(2,1)S(1)}, s32[]{:T(128)}, /*index=5*/s32[]{:T(128)}) %tuple.30), condition=%wide.while_cond, body=%wide.while_body.sunk | while | flops 2 | bytes 12401 | solution.py:33
  148.7 1.3 dynamic-slice.7
  150.7 1.3 dynamic-slice.7
  152.8 1.3 dynamic-slice.7
  159.0 1.3 dynamic-slice.7
  161.0 1.3 dynamic-slice.7
  163.1 1.3 dynamic-slice.7
  169.3 1.3 dynamic-slice.7
  171.4 1.3 dynamic-slice.7
  173.4 1.3 dynamic-slice.7
  177.6 1.3 dynamic-slice.7
  179.6 1.3 dynamic-slice.7
  181.7 1.3 dynamic-slice.7
  187.9 1.3 dynamic-slice.7
  189.9 1.3 dynamic-slice.7
  192.0 1.3 dynamic-slice.7
  198.2 1.3 dynamic-slice.7
  200.3 1.3 dynamic-slice.7
  202.3 1.3 dynamic-slice.7
  208.5 1.3 dynamic-slice.7
  210.6 1.3 dynamic-slice.7
  212.6 1.3 dynamic-slice.7
  216.8 1.3 dynamic-slice.7
  218.8 1.3 dynamic-slice.7
  220.9 1.3 dynamic-slice.7
  227.1 1.3 dynamic-slice.7
  229.1 1.3 dynamic-slice.7
  231.2 1.3 dynamic-slice.7
  237.4 1.3 dynamic-slice.7
  239.5 1.3 dynamic-slice.7
  241.5 1.3 dynamic-slice.7
  247.7 1.3 dynamic-slice.7
  249.8 1.3 dynamic-slice.7
  251.8 1.3 dynamic-slice.7
  256.0 1.3 dynamic-slice.7
  258.0 1.3 dynamic-slice.7
  260.1 1.3 dynamic-slice.7
  266.3 1.3 dynamic-slice.7
  268.4 1.3 dynamic-slice.7
  270.4 1.3 dynamic-slice.7
  276.6 1.3 dynamic-slice.7
  411.9 71.3 %fusion.9 = f32[1,128,897]{1,0,2:T(1,128)S(1)} fusion(bf16[1,128,1536]{1,0,2:T(2,128)(2,1)S(1)} %copy.17, bf16[128,1,640]{0,1,2:T(2,128)(2,1)S(1)} %copy.18), kind=kOutput, calls=%fused_computation.32 | convolution fusion | flops 146964480 | bytes 1016320 | tf_op jit(solution)/shard_map/conv_general_dilated | solution.py:16
  484.9 8.9 %reduce-scatter.2.cloned.1.call-done = f32[16,896]{1,0:T(8,128)} async-done(((f32[32,896]{1,0:T(8,128)}), f32[16,896]{1,0:T(8,128)}) %reduce-scatter.2.cloned.1.call-update) | async-done | bytes 57360 | tf_op jit(solution)/shard_map/reduce_scatter | solution.py:75
  (525 shorter events, 221.4 us)
Async XLA Ops:
  6.5 66.8 %all-gather.3.cloned.1.call-start = ((), (), s32[]{:S(2)}) async-start(), calls=%async_computation.1 | async-start | bytes 3612672 | tf_op jit(solution)/shard_map/all_gather | solution.py:51
  7.3 128.0 %all-gather.5.cloned.1.call-start = ((), (), s32[]{:S(2)}) async-start(), calls=%async_computation.2 | async-start | bytes 3612672 | tf_op jit(solution)/shard_map/all_gather | solution.py:52
  8.0 485.8 %reduce-scatter.2.cloned.1.call-start = ((), (), s32[]{:S(2)}) async-start(), calls=%async_computation.3 | async-start | bytes 172032 | tf_op jit(solution)/shard_map/reduce_scatter | solution.py:75
  73.3 61.9 %collective-permute-start = (bf16[1792,896]{1,0:T(8,128)(2,1)}, bf16[1792,896]{1,0:T(8,128)(2,1)}, u32[]{:S(2)}, u32[]{:S(2)}) collective-permute-start(bf16[1792,896]{1,0:T(8,128)(2,1)} %all-gather.3.cloned.1.call-done), channel_id=1, source_target_pairs={{1,0},{3,2},{5,4},{7,6},{9,8},{11,10},{13,12},{15,14},{17,16},{19,... | collective-permute-start | bytes 9633800 | tf_op jit(solution)/shard_map/ppermute | solution.py:12
  82.5 55.0 %copy-start = (bf16[1792,896]{1,0:T(8,128)(2,1)S(1)}, bf16[1792,896]{1,0:T(8,128)(2,1)}, u32[]{:S(2)}) copy-start(bf16[1792,896]{1,0:T(8,128)(2,1)} %all-gather.3.cloned.1.call-done) | copy-start | bytes 9633796
  140.7 5.2 %copy-start.4 = (pred[128]{0:T(512)(128)(4,1)S(1)}, pred[128]{0:T(512)(128)(4,1)}, u32[]{:S(2)}) copy-start(pred[128]{0:T(512)(128)(4,1)} %compare_and_fusion) | copy-start | bytes 388
  140.7 5.3 %copy-start.1 = (bf16[128,1536]{1,0:T(8,128)(2,1)S(1)}, bf16[128,1536]{1,0:T(8,128)(2,1)}, u32[]{:S(2)}) copy-start(bf16[128,1536]{1,0:T(8,128)(2,1)} %custom-call.2) | copy-start | bytes 1179652
  140.7 5.3 %copy-start.2 = (s32[128,2]{0,1:T(2,128)S(1)}, s32[128,2]{0,1:T(2,128)}, u32[]{:S(2)}) copy-start(s32[128,2]{0,1:T(2,128)} %pad_add_fusion) | copy-start | bytes 3076
  411.9 71.4 %copy-start.3 = (f32[128]{0:T(128)S(1)}, f32[128]{0:T(128)}, u32[]{:S(2)}) copy-start(f32[128]{0:T(128)} %sqrt.18) | copy-start | bytes 1540
Sparse Core Ops, SparseCore 0:
  9.5 63.7 all-gather.2
  75.5 59.6 all-gather.4
  485.0 8.7 reduce-scatter.1
where the time goes:
time: 503 us; the launch traced here: 500 us
  local copies, waits for them, and re-layouts  271 us (54%)
  waiting for transfers between devices  128 us (25%)
  matrix products  71.3 us (14%)
  between operations  13.3 us (3%)
  other arithmetic  11.5 us (2%)
    gather x512, local copies, waits for them, and re-layouts  261 us
    conv_general_dilated x1, matrix products, depthwise(): lax.conv_general_dilated(signal[None], kernel[:, None, :], (1,), 'VALID',...  71.3 us
    all_gather x1, waiting for transfers between devices, body(): lax.all_gather(samples, ('tmpl', 'chan'), axis=0, tiled=True)  65.3 us
    all_gather x1, waiting for transfers between devices, body(): lax.all_gather(tail, ('tmpl', 'chan'), axis=0, tiled=True)  52.7 us
  transfers between devices with their start and end apart: 4, of which 3 were waited for; matrix products, arithmetic and copies ran while one was open for 2% of the time, Pallas kernels for 0%

commit v1 on v0

v1 whole, which is shorter than its diff:
```python
import functools

import jax
import jax.numpy as jnp
from jax import lax
from jax.experimental import pallas as pl
from jax.experimental.pallas import tpu as pltpu
from jax.sharding import PartitionSpec as P

EPS = 1e-06
LANES = 128
GROUP = 8
STEP = 32
PIECES = LANES // STEP
VMEM_LIMIT = 60 * 1024 * 1024


def rolled(value, distance):
    size = value.shape[1]
    return pltpu.roll(value, (size - distance) % size, 1)


def window_kernel(length, samples_ref, rim_ref, wide_ref, scale_ref):
    block, rim = samples_ref.shape[1], rim_ref.shape[1]
    extent, starts = wide_ref.shape[1], scale_ref.shape[1]
    rows = 16

    @pl.loop(0, samples_ref.shape[0] // rows)
    def _(i):
        at = pl.ds(pl.multiple_of(i * rows, rows), rows)
        pieces = [samples_ref[at, :].astype(jnp.float32), rim_ref[at, :].astype(jnp.float32)]
        if extent > block + rim:
            pieces.append(jnp.zeros((rows, extent - block - rim), jnp.float32))
        wide = jnp.concatenate(pieces, axis=1)
        wide_ref[at, :] = wide
        total = wide * wide
        reach = 1
        while reach < LANES:
            total = total + rolled(total, reach)
            reach *= 2
        energy = total[:, :starts]
        for c in range(1, length // LANES):
            energy = energy + total[:, c * LANES : c * LANES + starts]
        scale_ref[at, :] = lax.rsqrt(energy + EPS)


def detect_kernel(
    groups_ref, slot_ref, row_ref, chan_ref, move_ref, weight_ref,
    waves_ref, wide_ref, scale_ref, out_ref,
    waves, picked, lined, shifts, spread, own, found,
):
    block = out_ref.shape[1]
    length = waves_ref.shape[1]
    count = length // STEP
    span = shifts.shape[1]
    taken = span + LANES
    scaled = block + LANES
    out_ref[...] = jnp.zeros_like(out_ref)

    @pl.loop(0, waves_ref.shape[0] // LANES)
    def _(i):
        at = pl.ds(pl.multiple_of(i * LANES, LANES), LANES)
        waves[at, :] = waves_ref[at, :].astype(jnp.float32)

    width = GROUP * STEP
    k_id = lax.broadcasted_iota(jnp.int32, (LANES, width), 0)
    r_id = lax.broadcasted_iota(jnp.int32, (LANES, width), 1) // GROUP
    for q in range(PIECES):
        spread[:, q * width : (q + 1) * width] = (k_id == r_id + q * STEP).astype(jnp.float32).astype(jnp.bfloat16)
    row_id = lax.broadcasted_iota(jnp.int32, (count // PIECES * GROUP, width), 0) % GROUP
    col_id = lax.broadcasted_iota(jnp.int32, (count // PIECES * GROUP, width), 1) % GROUP
    own[...] = (row_id == col_id).astype(jnp.float32)

    @pl.loop(0, groups_ref[0])
    def _(g):
        for i in range(GROUP):
            s = g * GROUP + i
            move = move_ref[s]
            coarse = pl.multiple_of((move // LANES) * LANES, LANES)
            fine = move % LANES
            picked[i : i + 1, :] = waves[pl.ds(slot_ref[s], 1), :]
            row = wide_ref[pl.ds(chan_ref[s], 1), pl.ds(coarse, taken)]
            lined[i : i + 1, :] = pltpu.roll(row, taken - fine, 1)
        wave = picked[...]
        tnorm = lax.rsqrt(jnp.sum(wave * wave, axis=1, keepdims=True) + EPS)
        for r in range(0, STEP, 2):
            pair = [rolled(lined[...], r + k)[:, :span] if r + k else lined[:, :span] for k in range(2)]
            shifts[r * GROUP : (r + 2) * GROUP, :] = jnp.concatenate(pair, axis=0).astype(jnp.bfloat16)
        blocks = count // PIECES
        stacked = jnp.concatenate([wave[:, j * LANES : (j + 1) * LANES] for j in range(blocks)], axis=0)
        expanded = jnp.dot(stacked.astype(jnp.bfloat16), spread[...], preferred_element_type=jnp.float32)
        mask = own[...]
        left = jnp.concatenate([expanded[:, q * width : (q + 1) * width] * mask for q in range(PIECES)], axis=0)
        product = jnp.dot(left.astype(jnp.bfloat16), shifts[...], preferred_element_type=jnp.float32)
        total = None
        for q in range(PIECES):
            part = None
            for j in range(blocks):
                at = (q * blocks + j) * GROUP
                term = product[at : at + GROUP, j * LANES : j * LANES + scaled]
                part = term if part is None else part + term
            if q:
                part = rolled(part, q * STEP)
            total = part if total is None else total + part
        found[...] = total[:, :block] * tnorm
        for i in range(GROUP):
            s = g * GROUP + i
            move = move_ref[s]
            coarse = pl.multiple_of((move // LANES) * LANES, LANES)
            fine = move % LANES
            scale = scale_ref[pl.ds(chan_ref[s], 1), pl.ds(coarse, scaled)]
            scale = pltpu.roll(scale, scaled - fine, 1)[:, :block]
            at = pl.ds(row_ref[s], 1)
            out_ref[at, :] += found[i : i + 1, :] * scale * weight_ref[s]


def vmem():
    return pl.BlockSpec(memory_space=pltpu.VMEM)


def smem():
    return pl.BlockSpec(memory_space=pltpu.SMEM)


def up(value, multiple):
    return -(-value // multiple) * multiple


def body(samples, tail, templates, channels, moveouts, live):
    chans, block = samples.shape
    per_dev, per_slot, length = templates.shape
    slots = per_dev * per_slot
    axes = ("tmpl", "chan")
    n_chan = lax.axis_size("chan")
    parts = lax.axis_size("tmpl") * n_chan
    me = lax.axis_index("tmpl") * n_chan + lax.axis_index("chan")
    n_rows = per_dev * lax.axis_size("tmpl")
    max_live, max_move = 64, 512

    slot_index = lax.axis_index("chan") * per_slot + jnp.arange(per_slot)
    code = (channels * max_move + moveouts) * max_live + live[:, None]
    code = jnp.where(slot_index[None, :] < live[:, None], code, -1).reshape(slots)
    codes = lax.all_gather(code, axes, axis=0, tiled=True)
    waveform = templates.reshape(slots, length)
    waves = lax.all_gather(waveform, axes, axis=0, tiled=True)

    devices = lax.axis_size("tm")
    route = [(i, i - 1) for i in range(1, devices)]
    following = lax.ppermute(samples, "tm", route)
    rim = jnp.where(lax.axis_index("tm") == devices - 1, tail[:, :block], following)

    padded = up(chans, 16)
    if padded != chans:
        samples = jnp.pad(samples, ((0, padded - chans), (0, 0)))
        rim = jnp.pad(rim, ((0, padded - chans), (0, 0)))
    starts = block + 3 * LANES
    extent = max(starts + length, block + rim.shape[1])
    wide, scale = pl.pallas_call(
        functools.partial(window_kernel, length),
        out_shape=(
            jax.ShapeDtypeStruct((padded, extent), jnp.float32),
            jax.ShapeDtypeStruct((padded, starts), jnp.float32),
        ),
        in_specs=[vmem(), vmem()],
        out_specs=(vmem(), vmem()),
        compiler_params=pltpu.CompilerParams(vmem_limit_bytes=VMEM_LIMIT),
    )(samples, rim)

    total = parts * slots
    index = jnp.arange(total)
    chan = codes // (max_move * max_live)
    mine = (codes >= 0) & (chan // chans == me)
    before = jnp.sum((index[None, :] < index[:, None]) & mine[None, :], axis=1, dtype=jnp.int32)
    number = jnp.sum(mine, dtype=jnp.int32)
    hit = (before[None, :] == index[:, None]) & mine[None, :]
    slot = jnp.sum(jnp.where(hit, index[None, :], 0), axis=1, dtype=jnp.int32)
    picked_code = jnp.sum(jnp.where(hit, codes[None, :], 0), axis=1, dtype=jnp.int32)
    used = index < number
    owner = slot // slots
    row = (owner // n_chan) * per_dev + (slot % slots) // per_slot
    local = jnp.where(used, picked_code // (max_move * max_live) - me * chans, 0)
    move = (picked_code // max_live) % max_move
    live_f = jnp.maximum(picked_code % max_live, 1).astype(jnp.float32)
    weight = jnp.where(used, jnp.sqrt(jnp.float32(length) / live_f), 0.0)
    groups = ((number + GROUP - 1) // GROUP).reshape(1)

    span = up(block + length - STEP, LANES)
    partial_value = pl.pallas_call(
        detect_kernel,
        out_shape=jax.ShapeDtypeStruct((n_rows, block), jnp.float32),
        in_specs=[smem()] * 6 + [vmem()] * 3,
        out_specs=vmem(),
        scratch_shapes=[
            pltpu.VMEM((total, length), jnp.float32),
            pltpu.VMEM((GROUP, length), jnp.float32),
            pltpu.VMEM((GROUP, span + LANES), jnp.float32),
            pltpu.VMEM((GROUP * STEP, span), jnp.bfloat16),
            pltpu.VMEM((LANES, PIECES * GROUP * STEP), jnp.bfloat16),
            pltpu.VMEM((length // LANES * GROUP, GROUP * STEP), jnp.float32),
            pltpu.VMEM((GROUP, block), jnp.float32),
        ],
        compiler_params=pltpu.CompilerParams(vmem_limit_bytes=VMEM_LIMIT),
    )(groups, slot, row, local, move, weight, waves, wide, scale)
    return lax.psum_scatter(partial_value, axes, scatter_dimension=0, tiled=True)


def solution(mesh):
    in_specs = (
        P(("tmpl", "chan"), ("groups", "tm")),
        P(("tmpl", "chan"), "groups"),
        P("tmpl", "chan", None),
        P("tmpl", "chan"),
        P("tmpl", "chan"),
        P("tmpl"),
    )
    out_specs = P(("tmpl", "chan"), ("groups", "tm"))
    return jax.shard_map(body, mesh=mesh, in_specs=in_specs, out_specs=out_specs, check_vma=False)
```

time: 503 us -> 137 us (0.27)
  local copies, waits for them, and re-layouts: 271 us -> 1.82 us
  matrix products: 71.3 us -> 0 us
  waiting for transfers between devices: 128 us -> 66.9 us
  Pallas kernels: 0 us -> 23.1 us
  blocking collectives: 0 us -> 22.1 us
    gather x514 -> x0, local copies, waits for them, and re-layouts: 266 us -> none
    all_gather x2 -> x1, waiting for transfers between devices: 118 us -> 4.78 us  [body(): waves = lax.all_gather(waveform, axes, axis=0, tiled=True)]
    conv_general_dilated x1 -> x0, matrix products: 71.3 us -> none  [depthwise(): lax.conv_general_dilated(signal[None], kernel[:, None, :], (1,), 'VALID',...]
    reduce_scatter x1, waiting for transfers between devices: 8.88 us -> 62.1 us  [body(): lax.psum_scatter(partial_value, axes, scatter_dimension=0, tiled=True)]
    pallas_call x0 -> x2, Pallas kernels: none -> 23.1 us  [the longest x1 13.4 us: body(): pl.pallas_call(detect_kernel, out_shape=jax.ShapeDtypeStruct((n_rows, blo...]
    all_gather x0 -> x1, blocking collectives: none -> 22.1 us  [body(): codes = lax.all_gather(code, axes, axis=0, tiled=True)]
  transfers between devices with their start and end apart: 4 -> 3, of which waited for: 3 -> 2; matrix products, arithmetic and copies ran while one was open for 2% -> 5% of each run, Pallas kernels for 0% -> 7%
where the time goes in v1:
time: 137 us
  waiting for transfers between devices  66.9 us (49%)
  Pallas kernels  23.1 us (17%)
  blocking collectives  22.1 us (16%)
  between operations  14.1 us (10%)
  other arithmetic  7.22 us (5%)
  local copies, waits for them, and re-layouts  1.82 us (1%)
    reduce_scatter x1, waiting for transfers between devices, body(): lax.psum_scatter(partial_value, axes, scatter_dimension=0, tiled=True)  62.1 us
    all_gather x1, blocking collectives, body(): codes = lax.all_gather(code, axes, axis=0, tiled=True)  22.1 us
    pallas_call x1, Pallas kernels, body(): pl.pallas_call(detect_kernel, out_shape=jax.ShapeDtypeStruct((n_rows, blo...  13.4 us
    pallas_call x1, Pallas kernels, body(): pl.pallas_call(functools.partial(window_kernel, length), out_shape=(jax.S...  9.68 us
    all_gather x1, waiting for transfers between devices, body(): waves = lax.all_gather(waveform, axes, axis=0, tiled=True)  4.78 us
  transfers between devices with their start and end apart: 3, of which 2 were waited for; matrix products, arithmetic and copies ran while one was open for 5% of the time, Pallas kernels for 7%

profile of v1, /device:TPU:0, one launch (start us, length us, event | category | flops | bytes accessed | tf_op | source)
XLA Modules:
  0.0 136.6 jit_solution(18337111737461455249)
XLA Ops:
  6.5 0.0 all-gather.3.cloned.1.call-start
  6.5 1.6 %reshape.19 = bf16[128,640]{1,0:T(8,128)(2,1)} reshape(bf16[32,4,640]{2,1,0:T(4,128)(2,1)} %param.8) | data formatting | bytes 327680 | tf_op jit(solution)/shard_map/reshape | solution.py:144
  8.2 0.0 all-gather.3.cloned.1.call-update
  8.2 0.0 reduce-scatter.2.cloned.1.call-start
  8.2 1.3 collective-permute-start
  9.6 0.8 add_select_fusion.10
  10.3 0.1 copy.10
  10.4 0.1 reshape.20
  10.5 22.1 %all-gather = s32[8,1,128]{2,1,0:T(1,128)S(1)} all-gather(s32[1,1,128]{2,1,0:T(1,128)S(1)} %reshape.20), channel_id=1, replica_groups=mesh['groups'=2,'tmpl'=4,'chan'=2,'tm'=2] {'tmpl','chan'}, dimensions={0}, use_global_device_ids=true | all-gather | bytes 4608 | tf_op jit(solution)/shard_map/all_gather | solution.py:143
  32.7 0.7 convert_reduce_fusion.1
  34.0 0.2 convert_reduce_fusion
  34.2 1.7 %select_reduce_fusion = (s32[1024]{0:T(1024)S(1)}, s32[1024]{0:T(1024)S(1)}) fusion(s32[1024]{0:T(1024)S(1)} %bitcast.3, s32[1024]{0:T(1024)S(1)} %convert_reduce_fusion, pred[1024]{0:T(1024)(128)(4,1)S(1)} %get-tuple-element.12), kind=kLoop, calls=%fused_computation | loop fusion | flops 6289408 | bytes 17408 | tf_op jit(solution)/shard_map/reduce_sum | solution.py:177
  35.9 0.0 copy-start
  35.9 1.2 fusion.16.weight_ref
  37.1 0.6 fusion.6.row_ref
  37.7 1.2 add_select_fusion.1
  39.0 0.0 collective-permute-done
  39.0 0.8 broadcast_select_fusion.rim_ref
  39.8 9.7 %shard_map.64 = (f32[224,1920]{1,0:T(8,128)}, f32[224,1280]{1,0:T(8,128)}) custom-call(bf16[224,896]{1,0:T(8,128)(2,1)} %samples_ref.1, bf16[224,896]{1,0:T(8,128)(2,1)} %broadcast_select_fusion.rim_ref), custom_call_target="tpu_custom_call" | custom-call | tf_op jit(solution)/shard_map/pallas_call | solution.py:158
  49.4 4.8 %all-gather.3.cloned.1.call-done.waves_ref = bf16[1024,640]{1,0:T(8,128)(2,1)} async-done(((bf16[128,640]{1,0:T(8,128)(2,1)}), bf16[1024,640]{1,0:T(8,128)(2,1)}) %all-gather.3.cloned.1.call-update) | async-done | bytes 1310736 | tf_op jit(solution)/shard_map/all_gather | solution.py:145
  54.2 0.0 copy-done
  54.2 13.4 %shard_map.65 = f32[128,896]{1,0:T(8,128)} custom-call(s32[1]{0:T(128)} %bitcast.1.groups_ref, s32[1024]{0:T(1024)} %copy-done, s32[1024]{0:T(1024)} %fusion.6.row_ref, s32[1024]{0:T(1024)} %get-tuple-element.14.chan_ref, s32[1024]{0:T(1024)} %get-tuple-element.13.move_ref, f32[1024]{0:T(1024)} %fusion.16.weight_ref, ...), custom_call_target="tpu_custom_call" | custom-call | tf_op jit(solution)/shard_map/pallas_call | solution.py:188
  67.7 0.0 reduce-scatter.2.cloned.1.call-update
  67.7 62.1 %reduce-scatter.2.cloned.1.call-done = f32[16,896]{1,0:T(8,128)} async-done(((f32[128,896]{1,0:T(8,128)}), f32[16,896]{1,0:T(8,128)}) %reduce-scatter.2.cloned.1.call-update) | async-done | bytes 57360 | tf_op jit(solution)/shard_map/reduce_scatter | solution.py:204
  (1 shorter events, 0.0 us)
Async XLA Ops:
  6.5 47.7 %all-gather.3.cloned.1.call-start = ((), (), s32[]{:S(2)}) async-start(), calls=%async_computation.1 | async-start | bytes 1474560 | tf_op jit(solution)/shard_map/all_gather | solution.py:145
  8.2 121.6 %reduce-scatter.2.cloned.1.call-start = ((), (), s32[]{:S(2)}) async-start(), calls=%async_computation.2 | async-start | bytes 516096 | tf_op jit(solution)/shard_map/reduce_scatter | solution.py:204
  8.2 30.7 %collective-permute-start = (bf16[224,896]{1,0:T(8,128)(2,1)}, bf16[224,896]{1,0:T(8,128)(2,1)S(1)}, u32[]{:S(2)}, u32[]{:S(2)}) collective-permute-start(bf16[224,896]{1,0:T(8,128)(2,1)} %samples_ref.1), channel_id=1, source_target_pairs={{1,0},{3,2},{5,4},{7,6},{9,8},{11,10},{13,12},{15,14},{17,16},{19,... | collective-permute-start | bytes 1204232 | tf_op jit(solution)/shard_map/ppermute | solution.py:149
  35.9 18.4 %copy-start = (s32[1024]{0:T(1024)}, s32[1024]{0:T(1024)S(1)}, u32[]{:S(2)}) copy-start(s32[1024]{0:T(1024)S(1)} %get-tuple-element.10.slot_ref) | copy-start | bytes 12292
Sparse Core Ops, SparseCore 0:
  9.5 44.6 all-gather.2
  67.8 61.9 reduce-scatter.1

commit v2 on v1

--- a/solution.py
+++ b/solution.py
@@ -114,6 +114,73 @@
             out_ref[at, :] += found[i : i + 1, :] * scale * weight_ref[s]
 
 
+def greet(peers):
+    barrier = pltpu.get_barrier_semaphore()
+    for peer in peers:
+        pl.semaphore_signal(barrier, inc=1, device_id=peer, device_id_type=pl.DeviceIdType.MESH)
+    pl.semaphore_wait(barrier, len(peers))
+
+
+def scatter_kernel(value_ref, out_ref, across, sums, along, x_send, x_recv, z_send, z_recv):
+    n_z, n_x = lax.axis_size("tmpl"), lax.axis_size("chan")
+    z, x = lax.axis_index("tmpl"), lax.axis_index("chan")
+    x_peers = [{"chan": lax.rem(x + j, n_x)} for j in range(1, n_x)]
+    z_peers = [{"tmpl": lax.rem(z + k, n_z)} for k in range(1, n_z)]
+    greet(x_peers + z_peers)
+    order = [*range(1, n_z), 0]
+    copies = {}
+    for k in order:
+        for j in range(1, n_x):
+            there = lax.rem(z + k, n_z) * n_x + lax.rem(x + j, n_x)
+            copies["x", k, j] = pltpu.make_async_remote_copy(
+                value_ref.at[there], across.at[k, j - 1], x_send.at[k, j - 1], x_recv.at[k, j - 1],
+                device_id=x_peers[j - 1], device_id_type=pl.DeviceIdType.MESH,
+            )
+            copies["x", k, j].start()
+    for k in order:
+        total = value_ref[lax.rem(z + k, n_z) * n_x + x]
+        for j in range(1, n_x):
+            copies["x", k, j].wait_recv()
+            total = total + across[k, j - 1]
+        sums[k] = total
+        if k:
+            copies["z", k] = pltpu.make_async_remote_copy(
+                sums.at[k], along.at[k - 1], z_send.at[k - 1], z_recv.at[k - 1],
+                device_id=z_peers[k - 1], device_id_type=pl.DeviceIdType.MESH,
+            )
+            copies["z", k].start()
+    total = sums[0]
+    for k in range(1, n_z):
+        copies["z", k].wait_recv()
+        total = total + along[k - 1]
+    out_ref[...] = total
+    for copy in copies.values():
+        copy.wait_send()
+
+
+def scattered(value):
+    n_z, n_x = lax.axis_size("tmpl"), lax.axis_size("chan")
+    keep, block = value.shape[0] // (n_z * n_x), value.shape[1]
+    return pl.pallas_call(
+        scatter_kernel,
+        out_shape=jax.ShapeDtypeStruct((keep, block), jnp.float32),
+        in_specs=[vmem()],
+        out_specs=vmem(),
+        scratch_shapes=[
+            pltpu.VMEM((n_z, n_x - 1, keep, block), jnp.float32),
+            pltpu.VMEM((n_z, keep, block), jnp.float32),
+            pltpu.VMEM((n_z - 1, keep, block), jnp.float32),
+            pltpu.SemaphoreType.DMA((n_z, n_x - 1)),
+            pltpu.SemaphoreType.DMA((n_z, n_x - 1)),
+            pltpu.SemaphoreType.DMA((n_z - 1,)),
+            pltpu.SemaphoreType.DMA((n_z - 1,)),
+        ],
+        compiler_params=pltpu.CompilerParams(
+            collective_id=1, has_side_effects=True, vmem_limit_bytes=VMEM_LIMIT
+        ),
+    )(value.reshape(n_z * n_x, keep, block))
+
+
 def vmem():
     return pl.BlockSpec(memory_space=pltpu.VMEM)
 
@@ -201,7 +268,7 @@
         ],
         compiler_params=pltpu.CompilerParams(vmem_limit_bytes=VMEM_LIMIT),
     )(groups, slot, row, local, move, weight, waves, wide, scale)
-    return lax.psum_scatter(partial_value, axes, scatter_dimension=0, tiled=True)
+    return scattered(partial_value)
 
 
 def solution(mesh):

time: 137 us -> 89.3 us (0.65)
  waiting for transfers between devices: 66.9 us -> 4.84 us
  Pallas kernels: 23.1 us -> 36 us
  local copies, waits for them, and re-layouts: 1.82 us -> 3.27 us
    reduce_scatter x1 -> x0, waiting for transfers between devices: 62.1 us -> none  [body(): lax.psum_scatter(partial_value, axes, scatter_dimension=0, tiled=True)]
    pallas_call x0 -> x1, Pallas kernels: none -> 12 us  [scattered(): pl.pallas_call(scatter_kernel, out_shape=jax.ShapeDtypeStruct((keep, bloc...]
    unnamed x3 -> x4, local copies, waits for them, and re-layouts: 0.11 us -> 1.55 us
  transfers between devices with their start and end apart: 3 -> 2, of which waited for: 2 -> 1; matrix products, arithmetic and copies ran while one was open for 5% -> 8% of each run, Pallas kernels for 7% -> 11%
where the time goes in v2:
time: 89.3 us; the launch traced here: 88.9 us
  Pallas kernels  36 us (40%)
  blocking collectives  22.1 us (25%)
  between operations  14.1 us (16%)
  other arithmetic  7.21 us (8%)
  waiting for transfers between devices  4.84 us (5%)
  local copies, waits for them, and re-layouts  3.27 us (4%)
  starting transfers between devices  1.29 us (1%)
    all_gather x1, blocking collectives, body(): codes = lax.all_gather(code, axes, axis=0, tiled=True)  22.1 us
    pallas_call x1, Pallas kernels, body(): pl.pallas_call(detect_kernel, out_shape=jax.ShapeDtypeStruct((n_rows, blo...  14.3 us
    pallas_call x1, Pallas kernels, scattered(): pl.pallas_call(scatter_kernel, out_shape=jax.ShapeDtypeStruct((keep, bloc...  12 us
    pallas_call x1, Pallas kernels, body(): pl.pallas_call(functools.partial(window_kernel, length), out_shape=(jax.S...  9.69 us
    all_gather x1, waiting for transfers between devices, body(): waves = lax.all_gather(waveform, axes, axis=0, tiled=True)  4.82 us
  transfers between devices with their start and end apart: 2, of which 1 were waited for; matrix products, arithmetic and copies ran while one was open for 8% of the time, Pallas kernels for 11%

profile of v2, /device:TPU:0, one launch (start us, length us, event | category | flops | bytes accessed | tf_op | source)
XLA Modules:
  0.0 88.9 jit_solution(2048470570188005669)
XLA Ops:
  6.5 0.0 all-gather.3.cloned.1.call-start
  6.5 1.6 %reshape.22 = bf16[128,640]{1,0:T(8,128)(2,1)} reshape(bf16[32,4,640]{2,1,0:T(4,128)(2,1)} %param.8) | data formatting | bytes 327680 | tf_op jit(solution)/shard_map/reshape | solution.py:211
  8.2 0.0 all-gather.3.cloned.1.call-update
  8.2 1.3 %collective-permute-start = (bf16[224,896]{1,0:T(8,128)(2,1)}, bf16[224,896]{1,0:T(8,128)(2,1)S(1)}, u32[]{:S(2)}, u32[]{:S(2)}) collective-permute-start(bf16[224,896]{1,0:T(8,128)(2,1)} %samples_ref.1), channel_id=1, source_target_pairs={{1,0},{3,2},{5,4},{7,6},{9,8},{11,10},{13,12},{15,14},{17,16},{19,... | collective-permute-start | bytes 1204232 | tf_op jit(solution)/shard_map/ppermute | solution.py:216
  9.5 0.8 add_select_fusion.10
  10.3 0.1 copy.10
  10.4 0.1 reshape.24
  10.5 22.1 %all-gather = s32[8,1,128]{2,1,0:T(1,128)S(1)} all-gather(s32[1,1,128]{2,1,0:T(1,128)S(1)} %reshape.24), channel_id=1, replica_groups=mesh['groups'=2,'tmpl'=4,'chan'=2,'tm'=2] {'tmpl','chan'}, dimensions={0}, use_global_device_ids=true | all-gather | bytes 4608 | tf_op jit(solution)/shard_map/all_gather | solution.py:210
  32.6 0.7 convert_reduce_fusion.1
  33.9 0.2 convert_reduce_fusion
  34.1 1.7 %select_reduce_fusion = (s32[1024]{0:T(1024)S(1)}, s32[1024]{0:T(1024)S(1)}) fusion(s32[1024]{0:T(1024)S(1)} %bitcast.5, s32[1024]{0:T(1024)S(1)} %convert_reduce_fusion, pred[1024]{0:T(1024)(128)(4,1)S(1)} %get-tuple-element.12), kind=kLoop, calls=%fused_computation | loop fusion | flops 6289408 | bytes 17408 | tf_op jit(solution)/shard_map/reduce_sum | solution.py:244
  35.8 0.0 copy-start
  35.8 1.2 %fusion.16.weight_ref = f32[1024]{0:T(1024)} fusion(s32[1024]{0:T(1024)S(1)} %get-tuple-element.9, s32[]{:T(128)} %get-tuple-element.11), kind=kLoop, calls=%fused_computation.51 | loop fusion | flops 16384 | bytes 8196 | tf_op jit(solution)/shard_map/jit(_where)/select_n | solution.py:251
  37.1 0.6 fusion.6.row_ref
  37.7 1.2 %add_select_fusion.1 = (s32[1024]{0:T(1024)}, s32[1024]{0:T(1024)}) fusion(s32[1024]{0:T(1024)S(1)} %get-tuple-element.9, s32[]{:T(128)S(6)} %mul.35, s32[]{:T(128)} %get-tuple-element.11), kind=kLoop, calls=%fused_computation.9 | loop fusion | flops 39936 | bytes 12296 | tf_op jit(solution)/shard_map/jit(remainder)/select_n | solution.py:249
  38.9 0.0 collective-permute-done
  38.9 0.8 broadcast_select_fusion.rim_ref
  39.7 9.7 %shard_map.64 = (f32[224,1920]{1,0:T(8,128)}, f32[224,1280]{1,0:T(8,128)}) custom-call(bf16[224,896]{1,0:T(8,128)(2,1)} %samples_ref.1, bf16[224,896]{1,0:T(8,128)(2,1)} %broadcast_select_fusion.rim_ref), custom_call_target="tpu_custom_call" | custom-call | tf_op jit(solution)/shard_map/pallas_call | solution.py:225
  49.4 4.8 %all-gather.3.cloned.1.call-done.waves_ref = bf16[1024,640]{1,0:T(8,128)(2,1)} async-done(((bf16[128,640]{1,0:T(8,128)(2,1)}), bf16[1024,640]{1,0:T(8,128)(2,1)}) %all-gather.3.cloned.1.call-update) | async-done | bytes 1310736 | tf_op jit(solution)/shard_map/all_gather | solution.py:212
  54.2 0.0 copy-done
  54.2 14.3 %shard_map.65 = f32[128,896]{1,0:T(8,128)} custom-call(s32[1]{0:T(128)} %bitcast.1.groups_ref, s32[1024]{0:T(1024)} %copy-done, s32[1024]{0:T(1024)} %fusion.6.row_ref, s32[1024]{0:T(1024)} %get-tuple-element.14.chan_ref, s32[1024]{0:T(1024)} %get-tuple-element.13.move_ref, f32[1024]{0:T(1024)} %fusion.16.weight_ref, ...), custom_call_target="tpu_custom_call" | custom-call | tf_op jit(solution)/shard_map/pallas_call | solution.py:255
  68.6 12.0 %shard_map.66 = f32[16,896]{1,0:T(8,128)} custom-call(f32[8,16,896]{2,1,0:T(8,128)} %bitcast.3), custom_call_target="tpu_custom_call" | custom-call | tf_op jit(solution)/shard_map/pallas_call | solution.py:164
  80.6 1.4 %copy.12 = f32[16,896]{1,0:T(8,128)} copy(f32[16,896]{1,0:T(8,128)} %shard_map.66) | data formatting | bytes 114688
  (1 shorter events, 0.0 us)
Async XLA Ops:
  6.5 47.7 %all-gather.3.cloned.1.call-start = ((), (), s32[]{:S(2)}) async-start(), calls=%async_computation | async-start | bytes 1474560 | tf_op jit(solution)/shard_map/all_gather | solution.py:212
  8.2 30.7 %collective-permute-start = (bf16[224,896]{1,0:T(8,128)(2,1)}, bf16[224,896]{1,0:T(8,128)(2,1)S(1)}, u32[]{:S(2)}, u32[]{:S(2)}) collective-permute-start(bf16[224,896]{1,0:T(8,128)(2,1)} %samples_ref.1), channel_id=1, source_target_pairs={{1,0},{3,2},{5,4},{7,6},{9,8},{11,10},{13,12},{15,14},{17,16},{19,... | collective-permute-start | bytes 1204232 | tf_op jit(solution)/shard_map/ppermute | solution.py:216
  35.8 18.4 %copy-start = (s32[1024]{0:T(1024)}, s32[1024]{0:T(1024)S(1)}, u32[]{:S(2)}) copy-start(s32[1024]{0:T(1024)S(1)} %get-tuple-element.10.slot_ref) | copy-start | bytes 12292
Sparse Core Ops, SparseCore 0:
  9.5 44.6 all-gather.2

commit v3 on v2

--- a/solution.py
+++ b/solution.py
@@ -10,6 +10,7 @@
 EPS = 1e-06
 LANES = 128
 GROUP = 8
+ROWS = 16
 STEP = 32
 PIECES = LANES // STEP
 VMEM_LIMIT = 60 * 1024 * 1024
@@ -20,17 +21,19 @@
     return pltpu.roll(value, (size - distance) % size, 1)
 
 
-def window_kernel(length, samples_ref, rim_ref, wide_ref, scale_ref):
-    block, rim = samples_ref.shape[1], rim_ref.shape[1]
+def window_rows(length, samples_ref, halo, tail_ref, is_last, wide_ref, scale_ref, first, last):
+    block, rim = samples_ref.shape[1], tail_ref.shape[1]
     extent, starts = wide_ref.shape[1], scale_ref.shape[1]
-    rows = 16
-
-    @pl.loop(0, samples_ref.shape[0] // rows)
+    if first == last:
+        return
+
+    @pl.loop(first, last)
     def _(i):
-        at = pl.ds(pl.multiple_of(i * rows, rows), rows)
-        pieces = [samples_ref[at, :].astype(jnp.float32), rim_ref[at, :].astype(jnp.float32)]
+        at = pl.ds(pl.multiple_of(i * ROWS, ROWS), ROWS)
+        after = jnp.where(is_last, tail_ref[at, :].astype(jnp.float32), halo[at, :].astype(jnp.float32))
+        pieces = [samples_ref[at, :].astype(jnp.float32), after]
         if extent > block + rim:
-            pieces.append(jnp.zeros((rows, extent - block - rim), jnp.float32))
+            pieces.append(jnp.zeros((ROWS, extent - block - rim), jnp.float32))
         wide = jnp.concatenate(pieces, axis=1)
         wide_ref[at, :] = wide
         total = wide * wide
@@ -42,6 +45,81 @@
         for c in range(1, length // LANES):
             energy = energy + total[:, c * LANES : c * LANES + starts]
         scale_ref[at, :] = lax.rsqrt(energy + EPS)
+
+
+def gather_kernel(
+    length, own_ref, code_ref, samples_ref, tail_ref,
+    waves_ref, codes_ref, wide_ref, scale_ref,
+    halo, halo_sems, code_send, code_recv, z_send, z_recv, x_send, x_recv, c_send, c_recv,
+):
+    n_z, n_x, n_c = (lax.axis_size(a) for a in ("tmpl", "chan", "tm"))
+    z, x, c = (lax.axis_index(a) for a in ("tmpl", "chan", "tm"))
+    me = z * n_x + x
+    share = own_ref.shape[0] // n_c
+    rows = pl.ds(pl.multiple_of(c * share, share), share)
+    far = [(k, j) for k in range(n_z) for j in range(n_x) if k or j]
+
+    def ahead(k, j):
+        return {"tmpl": lax.rem(z + k, n_z), "chan": lax.rem(x + j, n_x)}
+
+    def sibling(t):
+        return {"tm": lax.rem(c + t, n_c)}
+
+    greet([ahead(k, j) for k, j in far] + [sibling(t) for t in range(1, n_c)])
+    copies = {}
+
+    def send(name, source, target, send_sem, recv_sem, device):
+        copies[name] = pltpu.make_async_remote_copy(
+            source, target, send_sem, recv_sem, device_id=device, device_id_type=pl.DeviceIdType.MESH
+        )
+        copies[name].start()
+
+    def pass_x(k, source, target):
+        for j in range(1, n_x):
+            send(("x", k, j), source, target, x_send.at[k, j - 1], x_recv.at[k, j - 1], ahead(0, j))
+
+    def pass_core(k, j):
+        at = lax.rem(z - k + n_z, n_z) * n_x + lax.rem(x - j + n_x, n_x)
+        block = waves_ref.at[at, rows]
+        for t in range(1, n_c):
+            send(
+                ("c", k, j, t), block, block, c_send.at[k * n_x + j, t - 1], c_recv.at[k * n_x + j, t - 1], sibling(t)
+            )
+
+    send("halo", samples_ref, halo, halo_sems.at[0], halo_sems.at[1], sibling(n_c - 1))
+    for k in range(1, n_z):
+        send(("z", k), own_ref.at[rows], waves_ref.at[me, rows], z_send.at[k - 1], z_recv.at[k - 1], ahead(k, 0))
+    pass_x(0, own_ref.at[rows], waves_ref.at[me, rows])
+    for k, j in far:
+        at = k * n_x + j
+        send(("code", k, j), code_ref, codes_ref.at[me], code_send.at[at], code_recv.at[at], ahead(k, j))
+    waves_ref[me] = own_ref[...]
+    codes_ref[me] = code_ref[...]
+    copies["halo"].wait_recv()
+
+    steps = samples_ref.shape[0] // ROWS
+    marks = [steps * i // (n_z + 1) for i in range(n_z + 2)]
+    window = functools.partial(
+        window_rows, length, samples_ref, halo, tail_ref, c == n_c - 1, wide_ref, scale_ref
+    )
+    for k in range(1, n_z):
+        window(marks[k - 1], marks[k])
+        copies["z", k].wait_recv()
+        block = waves_ref.at[lax.rem(z - k + n_z, n_z) * n_x + x, rows]
+        pass_x(k, block, block)
+        pass_core(k, 0)
+    window(marks[n_z - 1], marks[n_z])
+    for k in range(n_z):
+        for j in range(1, n_x):
+            copies["x", k, j].wait_recv()
+            pass_core(k, j)
+    window(marks[n_z], marks[n_z + 1])
+    for k, j in far:
+        copies["code", k, j].wait_recv()
+        for t in range(1, n_c):
+            copies["c", k, j, t].wait_recv()
+    for copy in copies.values():
+        copy.wait_send()
 
 
 def detect_kernel(
@@ -197,7 +275,6 @@
     chans, block = samples.shape
     per_dev, per_slot, length = templates.shape
     slots = per_dev * per_slot
-    axes = ("tmpl", "chan")
     n_chan = lax.axis_size("chan")
     parts = lax.axis_size("tmpl") * n_chan
     me = lax.axis_index("tmpl") * n_chan + lax.axis_index("chan")
@@ -207,31 +284,42 @@
     slot_index = lax.axis_index("chan") * per_slot + jnp.arange(per_slot)
     code = (channels * max_move + moveouts) * max_live + live[:, None]
     code = jnp.where(slot_index[None, :] < live[:, None], code, -1).reshape(slots)
-    codes = lax.all_gather(code, axes, axis=0, tiled=True)
     waveform = templates.reshape(slots, length)
-    waves = lax.all_gather(waveform, axes, axis=0, tiled=True)
-
-    devices = lax.axis_size("tm")
-    route = [(i, i - 1) for i in range(1, devices)]
-    following = lax.ppermute(samples, "tm", route)
-    rim = jnp.where(lax.axis_index("tm") == devices - 1, tail[:, :block], following)
-
-    padded = up(chans, 16)
+    padded = up(chans, ROWS)
     if padded != chans:
         samples = jnp.pad(samples, ((0, padded - chans), (0, 0)))
-        rim = jnp.pad(rim, ((0, padded - chans), (0, 0)))
+        tail = jnp.pad(tail, ((0, padded - chans), (0, 0)))
     starts = block + 3 * LANES
-    extent = max(starts + length, block + rim.shape[1])
-    wide, scale = pl.pallas_call(
-        functools.partial(window_kernel, length),
+    extent = max(starts + length, block + tail.shape[1])
+    n_z, n_c = lax.axis_size("tmpl"), lax.axis_size("tm")
+
+    def sems(*extent):
+        return [pltpu.SemaphoreType.DMA(extent)] * 2
+
+    waves, codes, wide, scale = pl.pallas_call(
+        functools.partial(gather_kernel, length),
         out_shape=(
+            jax.ShapeDtypeStruct((parts, slots, length), jnp.bfloat16),
+            jax.ShapeDtypeStruct((parts, 1, slots), jnp.int32),
             jax.ShapeDtypeStruct((padded, extent), jnp.float32),
             jax.ShapeDtypeStruct((padded, starts), jnp.float32),
         ),
-        in_specs=[vmem(), vmem()],
-        out_specs=(vmem(), vmem()),
-        compiler_params=pltpu.CompilerParams(vmem_limit_bytes=VMEM_LIMIT),
-    )(samples, rim)
+        in_specs=[vmem()] * 4,
+        out_specs=(vmem(),) * 4,
+        scratch_shapes=[
+            pltpu.VMEM((padded, block), jnp.bfloat16),
+            pltpu.SemaphoreType.DMA((2,)),
+            *sems(parts),
+            *sems(n_z - 1),
+            *sems(n_z, n_chan - 1),
+            *sems(parts, n_c - 1),
+        ],
+        compiler_params=pltpu.CompilerParams(
+            collective_id=2, has_side_effects=True, vmem_limit_bytes=VMEM_LIMIT
+        ),
+    )(waveform, code.reshape(1, slots), samples, tail)
+    waves = waves.reshape(parts * slots, length)
+    codes = codes.reshape(parts * slots)
 
     total = parts * slots
     index = jnp.arange(total)

time: 89.3 us -> 64.2 us (0.72)
  blocking collectives: 22.1 us -> 0 us
  Pallas kernels: 36 us -> 52 us
  between operations: 14.1 us -> 0.62 us
  waiting for transfers between devices: 4.84 us -> 0 us
  starting transfers between devices: 1.29 us -> 0 us
    all_gather x1 -> x0, blocking collectives: 22.1 us -> none  [body(): codes = lax.all_gather(code, axes, axis=0, tiled=True)]
    pallas_call x1, Pallas kernels: 9.69 us -> 22.8 us  [body(): pl.pallas_call(functools.partial(gather_kernel, length), out_shape=(jax.S...]
    all_gather x1 -> x0, waiting for transfers between devices: 4.82 us -> none  [body(): waves = lax.all_gather(waveform, axes, axis=0, tiled=True)]
    pallas_call x1, Pallas kernels: 12 us -> 15.8 us  [scattered(): pl.pallas_call(scatter_kernel, out_shape=jax.ShapeDtypeStruct((keep, bloc...]
    ppermute x1 -> x0, starting transfers between devices: 1.29 us -> none  [body(): following = lax.ppermute(samples, 'tm', route)]
  transfers between devices with their start and end apart: 2 -> 0, of which waited for: 1 -> 0; matrix products, arithmetic and copies ran while one was open for 8% -> 0% of each run, Pallas kernels for 11% -> 0%
where the time goes in v3:
time: 64.2 us; the launch traced here: 64.3 us
  Pallas kernels  52 us (81%)
  other arithmetic  7.83 us (12%)
  local copies, waits for them, and re-layouts  3.78 us (6%)
    pallas_call x1, Pallas kernels, body(): pl.pallas_call(functools.partial(gather_kernel, length), out_shape=(jax.S...  22.8 us
    pallas_call x1, Pallas kernels, scattered(): pl.pallas_call(scatter_kernel, out_shape=jax.ShapeDtypeStruct((keep, bloc...  15.8 us
    pallas_call x1, Pallas kernels, body(): pl.pallas_call(detect_kernel, out_shape=jax.ShapeDtypeStruct((n_rows, blo...  13.4 us
    reduce_sum x1, other arithmetic, body(): jnp.sum(jnp.where(hit, codes[None, :], 0), axis=1, dtype=jnp.int32)  2.41 us
    reshape x1, local copies, waits for them, and re-layouts, body(): waveform = templates.reshape(slots, length)  1.62 us
    unnamed x3, local copies, waits for them, and re-layouts  1.45 us
    reduce_sum x1, other arithmetic, body(): number = jnp.sum(mine, dtype=jnp.int32)  1.37 us

profile of v3, /device:TPU:0, one launch (start us, length us, event | category | flops | bytes accessed | tf_op | source)
XLA Modules:
  0.0 64.3 jit_solution(14420632965806984483)
XLA Ops:
  0.0 0.8 %add_select_fusion.10 = s32[32,4]{0,1:T(4,128)S(1)} fusion(s32[32,4]{0,1:T(4,128)} %param.10, s32[32,4]{0,1:T(4,128)} %param.9, s32[32]{0:T(128)} %param.11, s32[4]{0:T(128)S(1)} %iota_add_fusion), kind=kLoop, calls=%fused_computation.75 | loop fusion | flops 768 | bytes 1680 | tf_op jit(solution)/shard_map/jit(_where)/select_n | solution.py:286
  0.8 0.1 copy.9
  0.9 0.6 reshape_reshape.3.code_ref
  1.5 1.6 %reshape.64.own_ref = bf16[128,640]{1,0:T(8,128)(2,1)} reshape(bf16[32,4,640]{2,1,0:T(4,128)(2,1)} %param.8) | data formatting | bytes 327680 | tf_op jit(solution)/shard_map/reshape | solution.py:287
  3.1 22.8 %shard_map.64 = (bf16[8,128,640]{2,1,0:T(8,128)(2,1)}, s32[8,1,128]{2,1,0:T(1,128)}, f32[224,1920]{1,0:T(8,128)}, f32[224,1280]{1,0:T(8,128)}) custom-call(bf16[128,640]{1,0:T(8,128)(2,1)} %reshape.64.own_ref, s32[1,128]{1,0:T(1,128)} %reshape_reshape.3.code_ref, bf16[224,896]{1,0:T(8,128)(2,1)} %samples_ref.1, bf16[224,896]{1,0:T(8,128)(2,1)} %tail_ref.1), custom_call_target="tpu_custom_call" | custom-call | tf_op jit(solution)/shard_map/pallas_call | solution.py:299
  25.9 1.4 %fusion.17 = s32[]{:T(128)} fusion(s32[8,1,128]{2,1,0:T(1,128)} %get-tuple-element.9, s32[]{:T(128)S(6)} %add.65), kind=kLoop, calls=%fused_computation.65 | loop fusion | flops 28671 | bytes 4104 | tf_op jit(solution)/shard_map/reduce_sum | solution.py:329
  27.9 0.7 %compare_and_fusion = pred[1024]{0:T(1024)(128)(4,1)S(1)} fusion(s32[1024]{0:T(1024)} %bitcast.6, s32[]{:T(128)S(6)} %add.65), kind=kLoop, calls=%fused_computation.73 | loop fusion | flops 26624 | bytes 5124 | tf_op jit(solution)/shard_map/and | solution.py:327
  28.6 0.2 convert_reduce_fusion
  28.8 2.4 %select_reduce_fusion = (s32[1024]{0:T(1024)S(1)}, s32[1024]{0:T(1024)S(1)}) fusion(s32[1024]{0:T(1024)} %bitcast.7, s32[1024]{0:T(1024)S(1)} %convert_reduce_fusion, pred[1024]{0:T(1024)(128)(4,1)S(1)} %compare_and_fusion), kind=kLoop, calls=%fused_computation | loop fusion | flops 6289408 | bytes 17408 | tf_op jit(solution)/shard_map/reduce_sum | solution.py:332
  31.2 0.0 copy-start
  31.2 1.2 %fusion.16.weight_ref = f32[1024]{0:T(1024)} fusion(s32[1024]{0:T(1024)S(1)} %get-tuple-element.13, s32[]{:T(128)} %fusion.17), kind=kLoop, calls=%fused_computation.56 | loop fusion | flops 16384 | bytes 8196 | tf_op jit(solution)/shard_map/jit(_where)/select_n | solution.py:339
  32.4 1.2 %add_select_fusion.1 = (s32[1024]{0:T(1024)}, s32[1024]{0:T(1024)}, s32[1024]{0:T(1024)}) fusion(s32[1024]{0:T(1024)S(1)} %get-tuple-element.13, s32[]{:T(128)S(6)} %mul.35, s32[]{:T(128)} %fusion.17, s32[1024]{0:T(1024)S(1)} %get-tuple-element.14.slot_ref), kind=kLoop, calls=%fused_computation.14 | loop fusion | flops 92160 | bytes 20488 | tf_op jit(solution)/shard_map/jit(remainder)/select_n | solution.py:337
  33.6 0.0 copy-done
  33.6 13.4 %shard_map.65 = f32[128,896]{1,0:T(8,128)} custom-call(s32[1]{0:T(128)} %bitcast.groups_ref, s32[1024]{0:T(1024)} %copy-done, s32[1024]{0:T(1024)} %get-tuple-element.17.row_ref, s32[1024]{0:T(1024)} %get-tuple-element.16.chan_ref, s32[1024]{0:T(1024)} %get-tuple-element.15.move_ref, f32[1024]{0:T(1024)} %fusion.16.weight_ref, bf16[1024,640]{1,0:T(8,128)(2,1)} %bitcast.5, ...), custom_call_target="tpu_custom_call" | custom-call | tf_op jit(solution)/shard_map/pallas_call | solution.py:343
  47.0 15.8 %shard_map.66 = f32[16,896]{1,0:T(8,128)} custom-call(f32[8,16,896]{2,1,0:T(8,128)} %bitcast.4), custom_call_target="tpu_custom_call" | custom-call | tf_op jit(solution)/shard_map/pallas_call | solution.py:242
  62.8 1.4 %copy.11 = f32[16,896]{1,0:T(8,128)} copy(f32[16,896]{1,0:T(8,128)} %shard_map.66) | data formatting | bytes 114688
  (1 shorter events, 0.0 us)
Async XLA Ops:
  31.2 2.4 %copy-start = (s32[1024]{0:T(1024)}, s32[1024]{0:T(1024)S(1)}, u32[]{:S(2)}) copy-start(s32[1024]{0:T(1024)S(1)} %get-tuple-element.14.slot_ref) | copy-start | bytes 12292
